TPU v7x, 32 devices: a whole 2x2x4 slice. The times are simulated.
32 devices in a mesh: section: 4 (over z), tm: 4 (over y, x), batch: 2 (over core).
Axes of the slice: x: 2, y: 2, z: 4, core: 2. Of those that a mesh axis runs over, the one named last changes fastest.
Arguments:
- acts: bfloat16 [4, 4, 8, 6, 10240], P('section', 'batch', 'tm'), may hold values from -6 to 6
- cot: bfloat16 [4, 8, 6, 10240], P('batch', 'tm'), may hold values from -6 to 6
- spatial_weight: bfloat16 [4, 9, 64, 64], P('section'), may hold values from -0.25 to 0.25
- temporal_weight: bfloat16 [4, 3, 64, 64], P('section'), may hold values from -0.4375 to 0.4375
Outputs:
- grad_in: bfloat16 [4, 4, 8, 6, 10240], P('section', 'batch', 'tm')
- grad_spatial: float32 [4, 9, 64, 64], P('section')
- grad_temporal: float32 [4, 3, 64, 64], P('section')
All inputs are finite; a program needn't handle non-finite values.
Results may differ from a plain program's by a relative error of at most 0.012.
Values may be sent and summed in bfloat16 or wider, within the bound.
A program may use at most 128 MiB of HBM per device.

v0:
```python
import jax
import jax.numpy as jnp
from jax import lax
from jax.sharding import PartitionSpec as P

TIME_DILATION = 2


def from_behind(value, axis, steps):
    count = lax.axis_size(axis)
    first, last = (max(0, -steps), min(count, count - steps))
    return lax.ppermute(value, axis, [(source, source + steps) for source in range(first, last)])


def split_pixels(a, chans):
    return a.reshape(a.shape[:-1] + (a.shape[-1] // chans, chans))


def paired_kernel(kernel):
    return jnp.kron(jnp.eye(2, dtype=kernel.dtype), kernel)


def spatial_fwd(x, ws):
    rows, width = (x.shape[1], x.shape[2])
    chans = ws.shape[-1]
    padded = jnp.pad(x, ((0, 0), (1, 1), (chans, chans)))
    total = jnp.zeros(x.shape, jnp.float32)
    for i in range(3):
        for j in range(3):
            piece = split_pixels(padded[:, i : i + rows, j * chans : j * chans + width], 2 * chans)
            total = total + jnp.einsum(
                "nrpa,ab->nrpb",
                piece,
                paired_kernel(ws[3 * i + j]),
                preferred_element_type=jnp.float32,
            ).reshape(x.shape)
    return total


def spatial_back(gz, x, ws):
    rows, width = (x.shape[1], x.shape[2])
    chans = ws.shape[-1]
    xpad = jnp.pad(x, ((0, 0), (1, 1), (chans, chans)))
    gradient_padded = jnp.pad(gz, ((0, 0), (1, 1), (chans, chans)))
    gz_pairs = split_pixels(gz, 2 * chans)
    total = jnp.zeros(x.shape, jnp.float32)
    grads = []
    for i in range(3):
        for j in range(3):
            gpiece = split_pixels(
                gradient_padded[:, 2 - i : 2 - i + rows, (2 - j) * chans : (2 - j) * chans + width],
                2 * chans,
            )
            total = total + jnp.einsum(
                "nrpb,ab->nrpa",
                gpiece,
                paired_kernel(ws[3 * i + j]),
                preferred_element_type=jnp.float32,
            ).reshape(x.shape)
            xpiece = split_pixels(xpad[:, i : i + rows, j * chans : j * chans + width], 2 * chans)
            square = jnp.einsum(
                "nrpa,nrpb->ab", xpiece, gz_pairs, preferred_element_type=jnp.float32
            )
            grads.append(square[:chans, :chans] + square[chans:, chans:])
    return (total, jnp.stack(grads))


def temporal_back(h, gradient_piece, gradient_padded, dilation_step, wt):
    count = gradient_piece.shape[0]
    chans = wt.shape[-1]
    kernel_taps = [
        gradient_padded[2 * dilation_step : 2 * dilation_step + count],
        gradient_piece,
        gradient_padded[0:count],
    ]
    h_pix = split_pixels(h, chans)
    gh = jnp.zeros(gradient_piece.shape, jnp.float32)
    tgrads = []
    for k in range(3):
        tap = split_pixels(kernel_taps[k], chans)
        gh = gh + jnp.einsum(
            "trwd,cd->trwc", tap, wt[k], preferred_element_type=jnp.float32
        ).reshape(gradient_piece.shape)
        tgrads.append(jnp.einsum("trwc,trwd->cd", h_pix, tap, preferred_element_type=jnp.float32))
    return (gh.astype(jnp.bfloat16), jnp.stack(tgrads))


def section_backward(x, gradient_piece, ws, wt):
    dilation_step = TIME_DILATION
    z = spatial_fwd(x, ws)
    sig = jax.nn.sigmoid(z)
    h = (z * sig).astype(jnp.bfloat16)
    deriv = sig * (1.0 + z * (1.0 - sig))
    tile_gradient, h_tile = (
        lax.all_to_all(gradient_piece, "tm", split_axis=2, concat_axis=0, tiled=True),
        lax.all_to_all(h, "tm", split_axis=2, concat_axis=0, tiled=True),
    )
    gradient_padded = jnp.pad(tile_gradient, ((dilation_step, dilation_step), (0, 0), (0, 0)))
    gh_tile, tgrads = temporal_back(h_tile, tile_gradient, gradient_padded, dilation_step, wt)
    gh = lax.all_to_all(gh_tile, "tm", split_axis=0, concat_axis=2, tiled=True)
    gz = (gh.astype(jnp.float32) * deriv).astype(jnp.bfloat16)
    back, sgrads = spatial_back(gz, x, ws)
    result = (gradient_piece.astype(jnp.float32) + back).astype(jnp.bfloat16)
    return (result, sgrads, tgrads)


def body(acts, cot, spatial_weight, temporal_weight):
    section_idx = lax.axis_index("section")
    number_sections = lax.axis_size("section")
    micro = acts.shape[1]
    local_acts = acts[0]
    ws = spatial_weight[0]
    wt = temporal_weight[0]
    received = jnp.zeros(cot.shape[1:], jnp.bfloat16)
    grads_in = jnp.zeros(local_acts.shape, jnp.bfloat16)
    acc_spatial = jnp.zeros(ws.shape, jnp.float32)
    acc_temporal = jnp.zeros(wt.shape, jnp.float32)
    total_turns = micro + number_sections - 1
    for turn in range(total_turns):
        which = jnp.int32(turn) - (number_sections - 1 - section_idx)
        valid = jnp.logical_and(which >= 0, which < micro)
        clipped = jnp.clip(which, 0, micro - 1)
        x_now = lax.dynamic_index_in_dim(local_acts, clipped, 0, keepdims=False)
        top_grad = lax.dynamic_index_in_dim(cot, clipped, 0, keepdims=False)
        incoming = jnp.where(section_idx == number_sections - 1, top_grad, received)
        result, sgrads, tgrads = section_backward(x_now, incoming, ws, wt)
        weight = valid.astype(jnp.float32)
        acc_spatial = acc_spatial + weight * sgrads
        acc_temporal = acc_temporal + weight * tgrads
        select = (jnp.arange(micro, dtype=jnp.int32) == which)[:, None, None, None]
        grads_in = jnp.where(select, result[None], grads_in)
        if turn + 1 < total_turns:
            received = from_behind(result, "section", -1)
    sum_spatial, sum_temporal = lax.psum((acc_spatial, acc_temporal), ("tm", "batch"))
    return (grads_in[None], sum_spatial[None], sum_temporal[None])


def solution(mesh):
    in_specs = (
        P("section", "batch", "tm", None, None),
        P("batch", "tm", None, None),
        P("section", None, None, None),
        P("section", None, None, None),
    )
    out_specs = (
        P("section", "batch", "tm", None, None),
        P("section", None, None, None),
        P("section", None, None, None),
    )
    return jax.shard_map(body, mesh=mesh, in_specs=in_specs, out_specs=out_specs, check_vma=False)
```

profile of v0, /device:TPU:24, one launch (start us, length us, event | category | flops | bytes accessed | tf_op | source)
XLA Modules:
  0.0 929.5 jit_solution(14927379624928204376)
XLA Ops:
  126.4 13.6 %reshape.1686 = bf16[10240,2,6]{2,1,0:T(2,128)(2,1)} reshape(bf16[4,2,15360]{2,1,0:T(2,128)(2,1)} %all-to-all-done) | data formatting | bytes 491520
  140.0 10.6 %copy.624 = bf16[2,6,4,2560]{3,0,2,1:T(2,128)(2,1)S(1)} copy(bf16[2,6,4,2560]{1,0,3,2:T(2,128)(2,1)} %bitcast.1160) | data formatting | bytes 491520 | tf_op jit(solution)/shard_map/all_to_all | solution.py:95
  205.2 10.3 %copy.809 = bf16[2,6,10240]{1,0,2:T(2,128)(2,1)} copy(bf16[2,6,10240]{2,0,1:T(2,128)(2,1)} %get-tuple-element.11) | data formatting | bytes 491520 | tf_op jit(solution)/shard_map/convert_element_type | solution.py:92
  257.1 12.6 %reshape.1696 = bf16[10240,2,6]{2,1,0:T(2,128)(2,1)} reshape(bf16[4,2,15360]{2,1,0:T(2,128)(2,1)S(1)} %all-to-all-done.10) | data formatting | bytes 491520
  269.7 12.2 %copy.902 = bf16[2,6,4,2560]{3,2,0,1:T(4,128)(2,1)S(1)} copy(bf16[2,6,4,2560]{1,0,3,2:T(2,128)(2,1)} %bitcast.1162) | data formatting | bytes 491520 | tf_op jit(solution)/shard_map/all_to_all | solution.py:96
  283.3 12.6 %reshape.1688 = bf16[10240,2,6]{2,1,0:T(2,128)(2,1)} reshape(bf16[4,2,15360]{2,1,0:T(2,128)(2,1)S(1)} %all-to-all-done.2) | data formatting | bytes 491520
  296.0 10.2 %copy.652 = bf16[2,6,4,2560]{3,0,2,1:T(2,128)(2,1)S(1)} copy(bf16[2,6,4,2560]{1,0,3,2:T(2,128)(2,1)} %bitcast.1163) | data formatting | bytes 491520 | tf_op jit(solution)/shard_map/all_to_all | solution.py:95
  366.4 10.3 %copy.812 = bf16[2,6,10240]{1,0,2:T(2,128)(2,1)} copy(bf16[2,6,10240]{2,0,1:T(2,128)(2,1)} %get-tuple-element.9) | data formatting | bytes 491520 | tf_op jit(solution)/shard_map/convert_element_type | solution.py:92
  418.4 12.6 %reshape.1698 = bf16[10240,2,6]{2,1,0:T(2,128)(2,1)} reshape(bf16[4,2,15360]{2,1,0:T(2,128)(2,1)S(1)} %all-to-all-done.11) | data formatting | bytes 491520
  431.1 12.2 %copy.903 = bf16[2,6,4,2560]{3,2,0,1:T(4,128)(2,1)S(1)} copy(bf16[2,6,4,2560]{1,0,3,2:T(2,128)(2,1)} %bitcast.1165) | data formatting | bytes 491520 | tf_op jit(solution)/shard_map/all_to_all | solution.py:96
  444.7 12.6 %reshape.1690 = bf16[10240,2,6]{2,1,0:T(2,128)(2,1)} reshape(bf16[4,2,15360]{2,1,0:T(2,128)(2,1)S(1)} %all-to-all-done.4) | data formatting | bytes 491520
  457.3 10.2 %copy.680 = bf16[2,6,4,2560]{3,0,2,1:T(2,128)(2,1)S(1)} copy(bf16[2,6,4,2560]{1,0,3,2:T(2,128)(2,1)} %bitcast.1166) | data formatting | bytes 491520 | tf_op jit(solution)/shard_map/all_to_all | solution.py:95
  577.8 12.6 %reshape.1700 = bf16[10240,2,6]{2,1,0:T(2,128)(2,1)} reshape(bf16[4,2,15360]{2,1,0:T(2,128)(2,1)S(1)} %all-to-all-done.12) | data formatting | bytes 491520
  590.4 12.2 %copy.904 = bf16[2,6,4,2560]{3,2,0,1:T(4,128)(2,1)S(1)} copy(bf16[2,6,4,2560]{1,0,3,2:T(2,128)(2,1)} %bitcast.1168) | data formatting | bytes 491520 | tf_op jit(solution)/shard_map/all_to_all | solution.py:96
  604.0 12.6 %reshape.1692 = bf16[10240,2,6]{2,1,0:T(2,128)(2,1)} reshape(bf16[4,2,15360]{2,1,0:T(2,128)(2,1)S(1)} %all-to-all-done.6) | data formatting | bytes 491520
  616.6 10.2 %copy.708 = bf16[2,6,4,2560]{3,0,2,1:T(2,128)(2,1)S(1)} copy(bf16[2,6,4,2560]{1,0,3,2:T(2,128)(2,1)} %bitcast.1169) | data formatting | bytes 491520 | tf_op jit(solution)/shard_map/all_to_all | solution.py:95
  735.9 12.6 %reshape.1702 = bf16[10240,2,6]{2,1,0:T(2,128)(2,1)} reshape(bf16[4,2,15360]{2,1,0:T(2,128)(2,1)S(1)} %all-to-all-done.13) | data formatting | bytes 491520
  748.5 12.2 %copy.905 = bf16[2,6,4,2560]{3,2,0,1:T(4,128)(2,1)S(1)} copy(bf16[2,6,4,2560]{1,0,3,2:T(2,128)(2,1)} %bitcast.1171) | data formatting | bytes 491520 | tf_op jit(solution)/shard_map/all_to_all | solution.py:96
  762.1 12.6 %reshape.1694 = bf16[10240,2,6]{2,1,0:T(2,128)(2,1)} reshape(bf16[4,2,15360]{2,1,0:T(2,128)(2,1)S(1)} %all-to-all-done.8) | data formatting | bytes 491520
  774.7 10.2 %copy.736 = bf16[2,6,4,2560]{3,0,2,1:T(2,128)(2,1)S(1)} copy(bf16[2,6,4,2560]{1,0,3,2:T(2,128)(2,1)} %bitcast.1172) | data formatting | bytes 491520 | tf_op jit(solution)/shard_map/all_to_all | solution.py:95
  841.1 10.3 %copy.821 = bf16[2,6,10240]{1,0,2:T(2,128)(2,1)} copy(bf16[2,6,10240]{2,0,1:T(2,128)(2,1)} %get-tuple-element.3) | data formatting | bytes 491520 | tf_op jit(solution)/shard_map/convert_element_type | solution.py:92
  870.4 12.6 %reshape.1704 = bf16[10240,2,6]{2,1,0:T(2,128)(2,1)} reshape(bf16[4,2,15360]{2,1,0:T(2,128)(2,1)S(1)} %all-to-all-done.14) | data formatting | bytes 491520
  883.2 12.3 %copy.906 = bf16[2,6,4,2560]{3,2,0,1:T(4,128)(2,1)S(1)} copy(bf16[2,6,4,2560]{1,0,3,2:T(2,128)(2,1)} %bitcast.1174) | data formatting | bytes 491520 | tf_op jit(solution)/shard_map/all_to_all | solution.py:96
  897.0 23.7 %psum.15 = f32[1,3,64,64]{3,2,1,0:T(8,128)} all-reduce(f32[1,3,64,64]{3,2,1,0:T(8,128)S(1)} %fusion.170), channel_id=1, replica_groups=mesh['section'=4,'tm'=4,'batch'=2] {'tm','batch'}, use_global_device_ids=true, to_apply=%region_1.2 | all-reduce | flops 12288 | bytes 98304 | tf_op jit(solution)/shard_map/psum | solution.py:134
  (836 shorter events, 617.3 us)
Async XLA Ops:
  26.5 99.9 %all-to-all-start = ((bf16[4,2,15360]{2,1,0:T(2,128)(2,1)}), bf16[4,2,15360]{2,1,0:T(2,128)(2,1)}, u32[]{:S(2)}, u32[]{:S(2)}) async-start(bf16[4,2,15360]{2,1,0:T(2,128)(2,1)} %reshape.1685), calls=%async_computation | async-start | bytes 491520 | tf_op jit(solution)/shard_map/all_to_all | solution.py:95
  33.8 160.6 %copy-start.16 = (bf16[128,128,1,1]{1,0,2,3:T(8,128)(2,1)}, bf16[128,128,1,1]{1,0,2,3:T(8,128)(2,1)S(1)}, u32[]{:S(2)}) copy-start(bf16[128,128,1,1]{1,0,2,3:T(8,128)(2,1)S(1)} %reshape.1603) | copy-start | bytes 98308
  33.9 160.8 %copy-start.11 = (bf16[128,128,1,1]{1,0,2,3:T(8,128)(2,1)}, bf16[128,128,1,1]{1,0,2,3:T(8,128)(2,1)S(1)}, u32[]{:S(2)}) copy-start(bf16[128,128,1,1]{1,0,2,3:T(8,128)(2,1)S(1)} %reshape.1604) | copy-start | bytes 98308
  34.1 160.9 %copy-start.6 = (bf16[128,128,1,1]{1,0,2,3:T(8,128)(2,1)}, bf16[128,128,1,1]{1,0,2,3:T(8,128)(2,1)S(1)}, u32[]{:S(2)}) copy-start(bf16[128,128,1,1]{1,0,2,3:T(8,128)(2,1)S(1)} %reshape.1605) | copy-start | bytes 98308
  34.2 162.0 %copy-start.1 = (bf16[128,128,1,1]{1,0,2,3:T(8,128)(2,1)}, bf16[128,128,1,1]{1,0,2,3:T(8,128)(2,1)S(1)}, u32[]{:S(2)}) copy-start(bf16[128,128,1,1]{1,0,2,3:T(8,128)(2,1)S(1)} %reshape.1606) | copy-start | bytes 98308
  153.7 9.9 %all-to-all-start.1 = ((bf16[8,6,2560]{2,1,0:T(8,128)(2,1)}), bf16[8,6,2560]{2,1,0:T(8,128)(2,1)S(1)}, u32[]{:S(2)}, u32[]{:S(2)}) async-start(bf16[8,6,2560]{2,1,0:T(8,128)(2,1)} %reshape.1671), calls=%async_computation.1 | async-start | bytes 655360 | tf_op jit(solution)/shard_map/all_to_all | solution.py:100
  202.7 31.0 %collective-permute-start = (bf16[2,6,10240]{2,0,1:T(2,128)(2,1)S(1)}, bf16[2,6,10240]{2,0,1:T(2,128)(2,1)S(1)}, u32[]{:S(2)}, u32[]{:S(2)}) collective-permute-start(bf16[2,6,10240]{2,0,1:T(2,128)(2,1)S(1)} %add_convert_fusion.5), channel_id=1, source_target_pairs={{8,0},{16,8},{24,16},{9,1},{17,9},{25,17},{10,2},{18,10},{26,18},{... | collective-permute-start | bytes 737288 | tf_op jit(solution)/shard_map/ppermute | solution.py:12
  225.4 26.6 %all-to-all-start.10 = ((bf16[4,2,15360]{2,1,0:T(2,128)(2,1)}), bf16[4,2,15360]{2,1,0:T(2,128)(2,1)S(1)}, u32[]{:S(2)}, u32[]{:S(2)}) async-start(bf16[4,2,15360]{2,1,0:T(2,128)(2,1)} %reshape.1695), calls=%async_computation.10 | async-start | bytes 491520 | tf_op jit(solution)/shard_map/all_to_all | solution.py:96
  252.0 31.3 %all-to-all-start.2 = ((bf16[4,2,15360]{2,1,0:T(2,128)(2,1)}), bf16[4,2,15360]{2,1,0:T(2,128)(2,1)S(1)}, u32[]{:S(2)}, u32[]{:S(2)}) async-start(bf16[4,2,15360]{2,1,0:T(2,128)(2,1)} %reshape.1687), calls=%async_computation.2 | async-start | bytes 491520 | tf_op jit(solution)/shard_map/all_to_all | solution.py:95
  314.8 10.0 %all-to-all-start.3 = ((bf16[8,6,2560]{2,1,0:T(8,128)(2,1)}), bf16[8,6,2560]{2,1,0:T(8,128)(2,1)}, u32[]{:S(2)}, u32[]{:S(2)}) async-start(bf16[8,6,2560]{2,1,0:T(8,128)(2,1)} %reshape.1681), calls=%async_computation.3 | async-start | bytes 655360 | tf_op jit(solution)/shard_map/all_to_all | solution.py:100
  364.0 31.2 %collective-permute-start.1 = (bf16[2,6,10240]{2,0,1:T(2,128)(2,1)S(1)}, bf16[2,6,10240]{2,0,1:T(2,128)(2,1)S(1)}, u32[]{:S(2)}, u32[]{:S(2)}) collective-permute-start(bf16[2,6,10240]{2,0,1:T(2,128)(2,1)S(1)} %add_convert_fusion.4), channel_id=1, source_target_pairs={{8,0},{16,8},{24,16},{9,1},{17,9},{25,17},{10,2},{18,10},{26,18},{... | collective-permute-start | bytes 737288 | tf_op jit(solution)/shard_map/ppermute | solution.py:12
  386.6 26.9 %all-to-all-start.11 = ((bf16[4,2,15360]{2,1,0:T(2,128)(2,1)}), bf16[4,2,15360]{2,1,0:T(2,128)(2,1)S(1)}, u32[]{:S(2)}, u32[]{:S(2)}) async-start(bf16[4,2,15360]{2,1,0:T(2,128)(2,1)} %reshape.1697), calls=%async_computation.11 | async-start | bytes 491520 | tf_op jit(solution)/shard_map/all_to_all | solution.py:96
  413.6 31.1 %all-to-all-start.4 = ((bf16[4,2,15360]{2,1,0:T(2,128)(2,1)}), bf16[4,2,15360]{2,1,0:T(2,128)(2,1)S(1)}, u32[]{:S(2)}, u32[]{:S(2)}) async-start(bf16[4,2,15360]{2,1,0:T(2,128)(2,1)} %reshape.1689), calls=%async_computation.4 | async-start | bytes 491520 | tf_op jit(solution)/shard_map/all_to_all | solution.py:95
  476.2 10.0 %all-to-all-start.5 = ((bf16[8,6,2560]{2,1,0:T(8,128)(2,1)}), bf16[8,6,2560]{2,1,0:T(8,128)(2,1)}, u32[]{:S(2)}, u32[]{:S(2)}) async-start(bf16[8,6,2560]{2,1,0:T(8,128)(2,1)} %reshape.1682), calls=%async_computation.5 | async-start | bytes 655360 | tf_op jit(solution)/shard_map/all_to_all | solution.py:100
  523.5 30.9 %collective-permute-start.2 = (bf16[2,6,10240]{2,0,1:T(2,128)(2,1)S(1)}, bf16[2,6,10240]{2,0,1:T(2,128)(2,1)S(1)}, u32[]{:S(2)}, u32[]{:S(2)}) collective-permute-start(bf16[2,6,10240]{2,0,1:T(2,128)(2,1)S(1)} %add_convert_fusion.3), channel_id=1, source_target_pairs={{8,0},{16,8},{24,16},{9,1},{17,9},{25,17},{10,2},{18,10},{26,18},{... | collective-permute-start | bytes 737288 | tf_op jit(solution)/shard_map/ppermute | solution.py:12
  545.9 26.8 %all-to-all-start.12 = ((bf16[4,2,15360]{2,1,0:T(2,128)(2,1)}), bf16[4,2,15360]{2,1,0:T(2,128)(2,1)S(1)}, u32[]{:S(2)}, u32[]{:S(2)}) async-start(bf16[4,2,15360]{2,1,0:T(2,128)(2,1)} %reshape.1699), calls=%async_computation.12 | async-start | bytes 491520 | tf_op jit(solution)/shard_map/all_to_all | solution.py:96
  572.7 31.3 %all-to-all-start.6 = ((bf16[4,2,15360]{2,1,0:T(2,128)(2,1)}), bf16[4,2,15360]{2,1,0:T(2,128)(2,1)S(1)}, u32[]{:S(2)}, u32[]{:S(2)}) async-start(bf16[4,2,15360]{2,1,0:T(2,128)(2,1)} %reshape.1691), calls=%async_computation.6 | async-start | bytes 491520 | tf_op jit(solution)/shard_map/all_to_all | solution.py:95
  635.5 10.2 %all-to-all-start.7 = ((bf16[8,6,2560]{2,1,0:T(8,128)(2,1)}), bf16[8,6,2560]{2,1,0:T(8,128)(2,1)}, u32[]{:S(2)}, u32[]{:S(2)}) async-start(bf16[8,6,2560]{2,1,0:T(8,128)(2,1)} %reshape.1683), calls=%async_computation.7 | async-start | bytes 655360 | tf_op jit(solution)/shard_map/all_to_all | solution.py:100
  685.6 27.1 %collective-permute-start.3 = (bf16[2,6,10240]{2,0,1:T(2,128)(2,1)S(1)}, bf16[2,6,10240]{2,0,1:T(2,128)(2,1)S(1)}, u32[]{:S(2)}, u32[]{:S(2)}) collective-permute-start(bf16[2,6,10240]{2,0,1:T(2,128)(2,1)S(1)} %add_convert_fusion.2), channel_id=1, source_target_pairs={{8,0},{16,8},{24,16},{9,1},{17,9},{25,17},{10,2},{18,10},{26,18},{... | collective-permute-start | bytes 737288 | tf_op jit(solution)/shard_map/ppermute | solution.py:12
  707.7 23.3 %all-to-all-start.13 = ((bf16[4,2,15360]{2,1,0:T(2,128)(2,1)}), bf16[4,2,15360]{2,1,0:T(2,128)(2,1)S(1)}, u32[]{:S(2)}, u32[]{:S(2)}) async-start(bf16[4,2,15360]{2,1,0:T(2,128)(2,1)} %reshape.1701), calls=%async_computation.13 | async-start | bytes 491520 | tf_op jit(solution)/shard_map/all_to_all | solution.py:96
  731.0 31.1 %all-to-all-start.8 = ((bf16[4,2,15360]{2,1,0:T(2,128)(2,1)}), bf16[4,2,15360]{2,1,0:T(2,128)(2,1)S(1)}, u32[]{:S(2)}, u32[]{:S(2)}) async-start(bf16[4,2,15360]{2,1,0:T(2,128)(2,1)} %reshape.1693), calls=%async_computation.8 | async-start | bytes 491520 | tf_op jit(solution)/shard_map/all_to_all | solution.py:95
  788.7 9.9 %all-to-all-start.9 = ((bf16[8,6,2560]{2,1,0:T(8,128)(2,1)}), bf16[8,6,2560]{2,1,0:T(8,128)(2,1)S(1)}, u32[]{:S(2)}, u32[]{:S(2)}) async-start(bf16[8,6,2560]{2,1,0:T(8,128)(2,1)} %reshape.1684), calls=%async_computation.9 | async-start | bytes 655360 | tf_op jit(solution)/shard_map/all_to_all | solution.py:100
  793.0 127.7 %all-reduce.17.cloned.1.call-start = ((), (), s32[]{:S(2)}) async-start(), calls=%async_computation.15 | async-start | bytes 589824 | tf_op jit(solution)/shard_map/psum | solution.py:134
  861.3 9.1 all-to-all-start.14
  (175 other events, 2755.1 us)
Sparse Core Ops, SparseCore 0:
  820.6 53.1 all-reduce.16
where the time goes:
time: 944 us; the launch traced here: 930 us
  local copies, waits for them, and re-layouts  609 us (65%)
  matrix products  137 us (15%)
  starting transfers between devices  70 us (7%)
  other arithmetic  49 us (5%)
  blocking collectives  23.7 us (3%)
  waiting for transfers between devices  23.2 us (2%)
  between operations  17.9 us (2%)
    unnamed x379, local copies, waits for them, and re-layouts  229 us
    reshape x105, local copies, waits for them, and re-layouts, split_pixels(): return a.reshape(a.shape[:-1] + (a.shape[-1] // chans, chans))  112 us
    all_to_all x10, local copies, waits for them, and re-layouts, section_backward(): lax.all_to_all(h, 'tm', split_axis=2, concat_axis=0, tiled=True)  61.8 us
    dot_general x45, matrix products, spatial_back(): jnp.einsum('nrpa,nrpb->ab', xpiece, gz_pairs, preferred_element_type=jnp....  54.5 us
    all_to_all x10, local copies, waits for them, and re-layouts, section_backward(): lax.all_to_all(gradient_piece, 'tm', split_axis=2, concat_axis=0, tiled=T...  52.1 us
    convert_element_type x5, local copies, waits for them, and re-layouts, section_backward(): h = (z * sig).astype(jnp.bfloat16)  51.3 us
    select_n x5, local copies, waits for them, and re-layouts, body(): incoming = jnp.where(section_idx == number_sections - 1, top_grad, received)  40.8 us
    dot_general x45, matrix products, spatial_fwd(): jnp.einsum('nrpa,ab->nrpb', piece, paired_kernel(ws[3 * i + j]), preferre...  28.6 us
  transfers between devices with their start and end apart: 20, of which 6 were waited for; matrix products, arithmetic and copies ran while one was open for 48% of the time, Pallas kernels for 0%

commit v1 on v0

--- a/solution.py
+++ b/solution.py
@@ -93,7 +93,9 @@
     deriv = sig * (1.0 + z * (1.0 - sig))
     tile_gradient, h_tile = (
         lax.all_to_all(gradient_piece, "tm", split_axis=2, concat_axis=0, tiled=True),
-        lax.all_to_all(h, "tm", split_axis=2, concat_axis=0, tiled=True),
+        jnp.concatenate(
+            lax.all_to_all(jnp.stack(jnp.split(h, lax.axis_size("tm"), axis=2)), "tm", 0, 0), axis=0
+        ),
     )
     gradient_padded = jnp.pad(tile_gradient, ((dilation_step, dilation_step), (0, 0), (0, 0)))
     gh_tile, tgrads = temporal_back(h_tile, tile_gradient, gradient_padded, dilation_step, wt)

time: 944 us -> 768 us (0.81)
  local copies, waits for them, and re-layouts: 609 us -> 390 us
  other arithmetic: 49 us -> 74.8 us
  waiting for transfers between devices: 23.2 us -> 37.3 us
    unnamed x379 -> x285, local copies, waits for them, and re-layouts: 229 us -> 117 us
    all_to_all x10 -> x5, local copies, waits for them, and re-layouts: 61.8 us -> 4.63 us  [section_backward(): lax.all_to_all(jnp.stack(jnp.split(h, lax.axis_size('tm'), axis=2)), 'tm'...]
    convert_element_type x5 -> x0, local copies, waits for them, and re-layouts: 51.3 us -> none  [section_backward(): h = (z * sig).astype(jnp.bfloat16)]
    unnamed x40, other arithmetic: 24.6 us -> 45.6 us
    all_to_all x5, waiting for transfers between devices: 0.01 us -> 9.65 us  [section_backward(): lax.all_to_all(gradient_piece, 'tm', split_axis=2, concat_axis=0, tiled=T...]
    reshape x105 -> x100, local copies, waits for them, and re-layouts: 112 us -> 109 us  [split_pixels(): return a.reshape(a.shape[:-1] + (a.shape[-1] // chans, chans))]
  transfers between devices with their start and end apart: 20 -> 20, of which waited for: 6 -> 10; matrix products, arithmetic and copies ran while one was open for 48% -> 42% of each run, Pallas kernels for 0% -> 0%
where the time goes in v1:
time: 768 us; the launch traced here: 755 us
  local copies, waits for them, and re-layouts  390 us (51%)
  matrix products  140 us (18%)
  other arithmetic  74.8 us (10%)
  starting transfers between devices  71.3 us (9%)
  waiting for transfers between devices  37.3 us (5%)
  blocking collectives  24 us (3%)
  between operations  17.4 us (2%)
    unnamed x285, local copies, waits for them, and re-layouts  117 us
    reshape x100, local copies, waits for them, and re-layouts, split_pixels(): return a.reshape(a.shape[:-1] + (a.shape[-1] // chans, chans))  109 us
    dot_general x45, matrix products, spatial_back(): jnp.einsum('nrpa,nrpb->ab', xpiece, gz_pairs, preferred_element_type=jnp....  59 us
    all_to_all x10, local copies, waits for them, and re-layouts, section_backward(): lax.all_to_all(gradient_piece, 'tm', split_axis=2, concat_axis=0, tiled=T...  51.7 us
    unnamed x40, other arithmetic  45.6 us
    select_n x5, local copies, waits for them, and re-layouts, body(): incoming = jnp.where(section_idx == number_sections - 1, top_grad, received)  40.7 us
    dot_general x45, matrix products, spatial_fwd(): jnp.einsum('nrpa,ab->nrpb', piece, paired_kernel(ws[3 * i + j]), preferre...  28.6 us
    dot_general x45, matrix products, spatial_back(): jnp.einsum('nrpb,ab->nrpa', gpiece, paired_kernel(ws[3 * i + j]), preferr...  27.4 us
  transfers between devices with their start and end apart: 20, of which 10 were waited for; matrix products, arithmetic and copies ran while one was open for 42% of the time, Pallas kernels for 0%

profile of v1, /device:TPU:24, one launch (start us, length us, event | category | flops | bytes accessed | tf_op | source)
XLA Modules:
  0.0 754.8 jit_solution(11102432508037530175)
XLA Ops:
  8.3 8.1 %copy.603 = bf16[2,6,10240]{1,0,2:T(2,128)(2,1)} copy(bf16[2,6,10240]{2,0,1:T(2,128)(2,1)S(1)} %fusion.321) | data formatting | bytes 491520 | tf_op jit(solution)/shard_map/jit(_where)/select_n | solution.py:127
  16.5 10.0 %reshape.1660 = bf16[4,2,15360]{2,1,0:T(2,128)(2,1)} reshape(bf16[10240,2,6]{2,1,0:T(2,128)(2,1)} %bitcast.1179) | data formatting | bytes 491520
  26.4 4.6 all-to-all-start
  125.6 13.6 %reshape.1661 = bf16[10240,2,6]{2,1,0:T(2,128)(2,1)} reshape(bf16[4,2,15360]{2,1,0:T(2,128)(2,1)} %all-to-all-done) | data formatting | bytes 491520
  139.2 10.2 %copy.604 = bf16[2,6,4,2560]{3,0,2,1:T(2,128)(2,1)S(1)} copy(bf16[2,6,4,2560]{1,0,3,2:T(2,128)(2,1)} %bitcast.1180) | data formatting | bytes 491520 | tf_op jit(solution)/shard_map/all_to_all | solution.py:95
  152.5 4.7 all-to-all-start.1
  215.1 8.1 %copy.631 = bf16[2,6,10240]{1,0,2:T(2,128)(2,1)} copy(bf16[2,6,10240]{2,0,1:T(2,128)(2,1)S(1)} %broadcast_select_fusion.9) | data formatting | bytes 491520 | tf_op jit(solution)/shard_map/jit(_where)/select_n | solution.py:127
  223.3 9.9 %reshape.1662 = bf16[4,2,15360]{2,1,0:T(2,128)(2,1)} reshape(bf16[10240,2,6]{2,1,0:T(2,128)(2,1)} %bitcast.1185) | data formatting | bytes 491520
  242.7 12.6 %reshape.1663 = bf16[10240,2,6]{2,1,0:T(2,128)(2,1)} reshape(bf16[4,2,15360]{2,1,0:T(2,128)(2,1)S(1)} %all-to-all-done.2) | data formatting | bytes 491520
  255.3 10.2 %copy.632 = bf16[2,6,4,2560]{3,0,2,1:T(2,128)(2,1)S(1)} copy(bf16[2,6,4,2560]{1,0,3,2:T(2,128)(2,1)} %bitcast.1181) | data formatting | bytes 491520 | tf_op jit(solution)/shard_map/all_to_all | solution.py:95
  341.9 8.1 %copy.659 = bf16[2,6,10240]{1,0,2:T(2,128)(2,1)} copy(bf16[2,6,10240]{2,0,1:T(2,128)(2,1)S(1)} %broadcast_select_fusion.8) | data formatting | bytes 491520 | tf_op jit(solution)/shard_map/jit(_where)/select_n | solution.py:127
  350.1 9.9 %reshape.1664 = bf16[4,2,15360]{2,1,0:T(2,128)(2,1)} reshape(bf16[10240,2,6]{2,1,0:T(2,128)(2,1)} %bitcast.1186) | data formatting | bytes 491520
  369.5 12.6 %reshape.1665 = bf16[10240,2,6]{2,1,0:T(2,128)(2,1)} reshape(bf16[4,2,15360]{2,1,0:T(2,128)(2,1)S(1)} %all-to-all-done.4) | data formatting | bytes 491520
  382.1 10.2 %copy.660 = bf16[2,6,4,2560]{3,0,2,1:T(2,128)(2,1)S(1)} copy(bf16[2,6,4,2560]{1,0,3,2:T(2,128)(2,1)} %bitcast.1182) | data formatting | bytes 491520 | tf_op jit(solution)/shard_map/all_to_all | solution.py:95
  468.9 8.1 %copy.687 = bf16[2,6,10240]{1,0,2:T(2,128)(2,1)} copy(bf16[2,6,10240]{2,0,1:T(2,128)(2,1)S(1)} %broadcast_select_fusion.7) | data formatting | bytes 491520 | tf_op jit(solution)/shard_map/jit(_where)/select_n | solution.py:127
  477.0 9.9 %reshape.1666 = bf16[4,2,15360]{2,1,0:T(2,128)(2,1)} reshape(bf16[10240,2,6]{2,1,0:T(2,128)(2,1)} %bitcast.1187) | data formatting | bytes 491520
  496.4 12.6 %reshape.1667 = bf16[10240,2,6]{2,1,0:T(2,128)(2,1)} reshape(bf16[4,2,15360]{2,1,0:T(2,128)(2,1)S(1)} %all-to-all-done.6) | data formatting | bytes 491520
  509.0 10.2 %copy.688 = bf16[2,6,4,2560]{3,0,2,1:T(2,128)(2,1)S(1)} copy(bf16[2,6,4,2560]{1,0,3,2:T(2,128)(2,1)} %bitcast.1183) | data formatting | bytes 491520 | tf_op jit(solution)/shard_map/all_to_all | solution.py:95
  595.2 8.1 %copy.715 = bf16[2,6,10240]{1,0,2:T(2,128)(2,1)} copy(bf16[2,6,10240]{2,0,1:T(2,128)(2,1)S(1)} %broadcast_select_fusion.6) | data formatting | bytes 491520 | tf_op jit(solution)/shard_map/jit(_where)/select_n | solution.py:127
  603.4 9.9 %reshape.1668 = bf16[4,2,15360]{2,1,0:T(2,128)(2,1)} reshape(bf16[10240,2,6]{2,1,0:T(2,128)(2,1)} %bitcast.1188) | data formatting | bytes 491520
  622.8 12.6 %reshape.1669 = bf16[10240,2,6]{2,1,0:T(2,128)(2,1)} reshape(bf16[4,2,15360]{2,1,0:T(2,128)(2,1)S(1)} %all-to-all-done.8) | data formatting | bytes 491520
  635.4 10.2 %copy.716 = bf16[2,6,4,2560]{3,0,2,1:T(2,128)(2,1)S(1)} copy(bf16[2,6,4,2560]{1,0,3,2:T(2,128)(2,1)} %bitcast.1184) | data formatting | bytes 491520 | tf_op jit(solution)/shard_map/all_to_all | solution.py:95
  714.0 24.0 %psum.15 = f32[1,3,64,64]{3,2,1,0:T(8,128)} all-reduce(f32[1,3,64,64]{3,2,1,0:T(8,128)S(1)} %fusion.170), channel_id=1, replica_groups=mesh['section'=4,'tm'=4,'batch'=2] {'tm','batch'}, use_global_device_ids=true, to_apply=%region_1.2 | all-reduce | flops 12288 | bytes 98304 | tf_op jit(solution)/shard_map/psum | solution.py:136
  738.0 8.0 %all-reduce.17.cloned.1.call-done = f32[1,9,64,64]{3,2,1,0:T(8,128)} async-done(((f32[1,9,64,64]{3,2,1,0:T(8,128)}), f32[1,9,64,64]{3,2,1,0:T(8,128)}) %all-reduce.17.cloned.1.call-update) | async-done | bytes 147472 | tf_op jit(solution)/shard_map/psum | solution.py:136
  (742 shorter events, 490.5 us)
Async XLA Ops:
  26.4 99.2 %all-to-all-start = ((bf16[4,2,15360]{2,1,0:T(2,128)(2,1)}), bf16[4,2,15360]{2,1,0:T(2,128)(2,1)}, u32[]{:S(2)}, u32[]{:S(2)}) async-start(bf16[4,2,15360]{2,1,0:T(2,128)(2,1)} %reshape.1660), calls=%async_computation | async-start | bytes 491520 | tf_op jit(solution)/shard_map/all_to_all | solution.py:95
  33.0 158.8 %copy-start.16 = (bf16[128,128,1,1]{1,0,2,3:T(8,128)(2,1)}, bf16[128,128,1,1]{1,0,2,3:T(8,128)(2,1)S(1)}, u32[]{:S(2)}) copy-start(bf16[128,128,1,1]{1,0,2,3:T(8,128)(2,1)S(1)} %reshape.1578) | copy-start | bytes 98308
  33.1 160.0 %copy-start.11 = (bf16[128,128,1,1]{1,0,2,3:T(8,128)(2,1)}, bf16[128,128,1,1]{1,0,2,3:T(8,128)(2,1)S(1)}, u32[]{:S(2)}) copy-start(bf16[128,128,1,1]{1,0,2,3:T(8,128)(2,1)S(1)} %reshape.1579) | copy-start | bytes 98308
  33.2 160.1 %copy-start.6 = (bf16[128,128,1,1]{1,0,2,3:T(8,128)(2,1)}, bf16[128,128,1,1]{1,0,2,3:T(8,128)(2,1)S(1)}, u32[]{:S(2)}) copy-start(bf16[128,128,1,1]{1,0,2,3:T(8,128)(2,1)S(1)} %reshape.1580) | copy-start | bytes 98308
  33.4 160.3 %copy-start.1 = (bf16[128,128,1,1]{1,0,2,3:T(8,128)(2,1)}, bf16[128,128,1,1]{1,0,2,3:T(8,128)(2,1)S(1)}, u32[]{:S(2)}) copy-start(bf16[128,128,1,1]{1,0,2,3:T(8,128)(2,1)S(1)} %reshape.1581) | copy-start | bytes 98308
  152.5 10.3 %all-to-all-start.1 = ((bf16[8,6,2560]{2,1,0:T(8,128)(2,1)}), bf16[8,6,2560]{2,1,0:T(8,128)(2,1)S(1)}, u32[]{:S(2)}, u32[]{:S(2)}) async-start(bf16[8,6,2560]{2,1,0:T(8,128)(2,1)} %reshape.1646), calls=%async_computation.1 | async-start | bytes 655360 | tf_op jit(solution)/shard_map/all_to_all | solution.py:102
  199.6 33.6 %all-to-all-start.10 = ((bf16[4,2,6,2560]{3,1,2,0:T(2,128)(2,1)}), bf16[4,2,6,2560]{3,1,2,0:T(2,128)(2,1)S(1)}, u32[]{:S(2)}, u32[]{:S(2)}) async-start(bf16[4,2,6,2560]{3,1,2,0:T(2,128)(2,1)} %pad_maximum_fusion), calls=%async_computation.10 | async-start | bytes 491520 | tf_op jit(solution)/shard_map/all_to_all | solution.py:97
  205.2 9.7 %collective-permute-start = (bf16[2,6,10240]{2,0,1:T(2,128)(2,1)S(1)}, bf16[2,6,10240]{2,0,1:T(2,128)(2,1)S(1)}, u32[]{:S(2)}, u32[]{:S(2)}) collective-permute-start(bf16[2,6,10240]{2,0,1:T(2,128)(2,1)S(1)} %add_convert_fusion.5), channel_id=1, source_target_pairs={{8,0},{16,8},{24,16},{9,1},{17,9},{25,17},{10,2},{18,10},{26,18},{... | collective-permute-start | bytes 737288 | tf_op jit(solution)/shard_map/ppermute | solution.py:12
  233.2 9.5 %all-to-all-start.2 = ((bf16[4,2,15360]{2,1,0:T(2,128)(2,1)}), bf16[4,2,15360]{2,1,0:T(2,128)(2,1)S(1)}, u32[]{:S(2)}, u32[]{:S(2)}) async-start(bf16[4,2,15360]{2,1,0:T(2,128)(2,1)} %reshape.1662), calls=%async_computation.2 | async-start | bytes 491520 | tf_op jit(solution)/shard_map/all_to_all | solution.py:95
  274.2 9.9 %all-to-all-start.3 = ((bf16[8,6,2560]{2,1,0:T(8,128)(2,1)}), bf16[8,6,2560]{2,1,0:T(8,128)(2,1)}, u32[]{:S(2)}, u32[]{:S(2)}) async-start(bf16[8,6,2560]{2,1,0:T(8,128)(2,1)} %reshape.1656), calls=%async_computation.3 | async-start | bytes 655360 | tf_op jit(solution)/shard_map/all_to_all | solution.py:102
  304.6 55.4 %all-to-all-start.11 = ((bf16[4,2,6,2560]{3,1,2,0:T(2,128)(2,1)}), bf16[4,2,6,2560]{3,1,2,0:T(2,128)(2,1)}, u32[]{:S(2)}, u32[]{:S(2)}) async-start(bf16[4,2,6,2560]{3,1,2,0:T(2,128)(2,1)} %pad_maximum_fusion.1), calls=%async_computation.11 | async-start | bytes 491520 | tf_op jit(solution)/shard_map/all_to_all | solution.py:97
  329.9 11.8 %collective-permute-start.1 = (bf16[2,6,10240]{2,0,1:T(2,128)(2,1)S(1)}, bf16[2,6,10240]{2,0,1:T(2,128)(2,1)S(1)}, u32[]{:S(2)}, u32[]{:S(2)}) collective-permute-start(bf16[2,6,10240]{2,0,1:T(2,128)(2,1)S(1)} %add_convert_fusion.4), channel_id=1, source_target_pairs={{8,0},{16,8},{24,16},{9,1},{17,9},{25,17},{10,2},{18,10},{26,18},{... | collective-permute-start | bytes 737288 | tf_op jit(solution)/shard_map/ppermute | solution.py:12
  360.0 9.5 %all-to-all-start.4 = ((bf16[4,2,15360]{2,1,0:T(2,128)(2,1)}), bf16[4,2,15360]{2,1,0:T(2,128)(2,1)S(1)}, u32[]{:S(2)}, u32[]{:S(2)}) async-start(bf16[4,2,15360]{2,1,0:T(2,128)(2,1)} %reshape.1664), calls=%async_computation.4 | async-start | bytes 491520 | tf_op jit(solution)/shard_map/all_to_all | solution.py:95
  401.0 9.7 %all-to-all-start.5 = ((bf16[8,6,2560]{2,1,0:T(8,128)(2,1)}), bf16[8,6,2560]{2,1,0:T(8,128)(2,1)}, u32[]{:S(2)}, u32[]{:S(2)}) async-start(bf16[8,6,2560]{2,1,0:T(8,128)(2,1)} %reshape.1657), calls=%async_computation.5 | async-start | bytes 655360 | tf_op jit(solution)/shard_map/all_to_all | solution.py:102
  429.4 57.5 %all-to-all-start.12 = ((bf16[4,2,6,2560]{3,1,2,0:T(2,128)(2,1)}), bf16[4,2,6,2560]{3,1,2,0:T(2,128)(2,1)}, u32[]{:S(2)}, u32[]{:S(2)}) async-start(bf16[4,2,6,2560]{3,1,2,0:T(2,128)(2,1)} %pad_maximum_fusion.2), calls=%async_computation.12 | async-start | bytes 491520 | tf_op jit(solution)/shard_map/all_to_all | solution.py:97
  456.9 11.7 %collective-permute-start.2 = (bf16[2,6,10240]{2,0,1:T(2,128)(2,1)S(1)}, bf16[2,6,10240]{2,0,1:T(2,128)(2,1)S(1)}, u32[]{:S(2)}, u32[]{:S(2)}) collective-permute-start(bf16[2,6,10240]{2,0,1:T(2,128)(2,1)S(1)} %add_convert_fusion.3), channel_id=1, source_target_pairs={{8,0},{16,8},{24,16},{9,1},{17,9},{25,17},{10,2},{18,10},{26,18},{... | collective-permute-start | bytes 737288 | tf_op jit(solution)/shard_map/ppermute | solution.py:12
  486.9 9.5 %all-to-all-start.6 = ((bf16[4,2,15360]{2,1,0:T(2,128)(2,1)}), bf16[4,2,15360]{2,1,0:T(2,128)(2,1)S(1)}, u32[]{:S(2)}, u32[]{:S(2)}) async-start(bf16[4,2,15360]{2,1,0:T(2,128)(2,1)} %reshape.1666), calls=%async_computation.6 | async-start | bytes 491520 | tf_op jit(solution)/shard_map/all_to_all | solution.py:95
  527.9 9.9 %all-to-all-start.7 = ((bf16[8,6,2560]{2,1,0:T(8,128)(2,1)}), bf16[8,6,2560]{2,1,0:T(8,128)(2,1)}, u32[]{:S(2)}, u32[]{:S(2)}) async-start(bf16[8,6,2560]{2,1,0:T(8,128)(2,1)} %reshape.1658), calls=%async_computation.7 | async-start | bytes 655360 | tf_op jit(solution)/shard_map/all_to_all | solution.py:102
  558.3 54.9 %all-to-all-start.13 = ((bf16[4,2,6,2560]{3,1,2,0:T(2,128)(2,1)}), bf16[4,2,6,2560]{3,1,2,0:T(2,128)(2,1)}, u32[]{:S(2)}, u32[]{:S(2)}) async-start(bf16[4,2,6,2560]{3,1,2,0:T(2,128)(2,1)} %pad_maximum_fusion.3), calls=%async_computation.13 | async-start | bytes 491520 | tf_op jit(solution)/shard_map/all_to_all | solution.py:97
  583.6 11.3 %collective-permute-start.3 = (bf16[2,6,10240]{2,0,1:T(2,128)(2,1)S(1)}, bf16[2,6,10240]{2,0,1:T(2,128)(2,1)S(1)}, u32[]{:S(2)}, u32[]{:S(2)}) collective-permute-start(bf16[2,6,10240]{2,0,1:T(2,128)(2,1)S(1)} %add_convert_fusion.2), channel_id=1, source_target_pairs={{8,0},{16,8},{24,16},{9,1},{17,9},{25,17},{10,2},{18,10},{26,18},{... | collective-permute-start | bytes 737288 | tf_op jit(solution)/shard_map/ppermute | solution.py:12
  613.3 9.5 %all-to-all-start.8 = ((bf16[4,2,15360]{2,1,0:T(2,128)(2,1)}), bf16[4,2,15360]{2,1,0:T(2,128)(2,1)S(1)}, u32[]{:S(2)}, u32[]{:S(2)}) async-start(bf16[4,2,15360]{2,1,0:T(2,128)(2,1)} %reshape.1668), calls=%async_computation.8 | async-start | bytes 491520 | tf_op jit(solution)/shard_map/all_to_all | solution.py:95
  649.4 9.1 %all-to-all-start.9 = ((bf16[8,6,2560]{2,1,0:T(8,128)(2,1)}), bf16[8,6,2560]{2,1,0:T(8,128)(2,1)S(1)}, u32[]{:S(2)}, u32[]{:S(2)}) async-start(bf16[8,6,2560]{2,1,0:T(8,128)(2,1)} %reshape.1659), calls=%async_computation.9 | async-start | bytes 655360 | tf_op jit(solution)/shard_map/all_to_all | solution.py:102
  677.1 33.6 %all-to-all-start.14 = ((bf16[4,2,6,2560]{3,1,2,0:T(2,128)(2,1)}), bf16[4,2,6,2560]{3,1,2,0:T(2,128)(2,1)}, u32[]{:S(2)}, u32[]{:S(2)}) async-start(bf16[4,2,6,2560]{3,1,2,0:T(2,128)(2,1)} %pad_maximum_fusion.4), calls=%async_computation.14 | async-start | bytes 491520 | tf_op jit(solution)/shard_map/all_to_all | solution.py:97
  681.3 64.7 %all-reduce.17.cloned.1.call-start = ((), (), s32[]{:S(2)}) async-start(), calls=%async_computation.15 | async-start | bytes 589824 | tf_op jit(solution)/shard_map/psum | solution.py:136
  (133 other events, 1802.2 us)
Sparse Core Ops, SparseCore 0:
  691.5 54.4 all-reduce.16
